TPU v7x, 32 devices: a whole 2x2x4 slice. The times are simulated.
32 devices in a mesh: pair: 16 (over z, y, x), vir: 2 (over core).
Axes of the slice: x: 2, y: 2, z: 4, core: 2. Of those that a mesh axis runs over, the one named last changes fastest.
Arguments:
- amplitudes: bfloat16 [40960, 1024], P('pair', 'vir'), may hold values from -6 to 6
- cycle_ints: bfloat16 [40960, 1024], P('pair', 'vir'), may hold values from -6 to 6
- int_rows: bfloat16 [1024, 1024], P('pair', 'vir'), may hold values from -6 to 6
- row_dest: int32 [1024, 2], P('pair'), may hold values from 0 to 15, all different within a row; in each aligned block of 64 rows (0 to 63, 64 to 127, ...) at most 16 rows name the same one
- vir_energy: float32 [1024], P('vir'), may hold values from 0.5 to 4
- occ_energy: float32 [40960], P('pair'), may hold values from -2 to -0.2
Outputs:
- residual: bfloat16 [40960, 1024], P('pair', 'vir')
Inputs may be any that keep to these rules, and one draw needn't show every extreme that they name: `row_dest`: each integral row names 2 different pair groups; among the 64 rows of one pair group no group is named more than 16 times, a bound that some block reaches.
All inputs are finite; a program needn't handle non-finite values.
Results may differ from a plain program's by a relative error of at most 0.008.
Values may be sent and summed in bfloat16 or wider, within the bound.
A program may use at most 64 MiB of HBM per device.

v0:
```python
import math
import jax
import jax.numpy as jnp
from jax import lax
from jax.sharding import PartitionSpec as P

SLOTS = 256


def dispatch(int_rows, row_dest, groups, capacity):
    rows = int_rows.shape[0]
    group = jnp.arange(groups, dtype=jnp.int32)
    member = jnp.any(row_dest[None, :, :] == group[:, None, None], axis=2)
    before = jnp.arange(rows)[:, None] < jnp.arange(rows)[None, :]
    rank = jnp.dot(
        member.astype(jnp.bfloat16), before.astype(jnp.bfloat16), preferred_element_type=jnp.float32
    ).astype(jnp.int32)
    slot = jnp.arange(capacity, dtype=jnp.int32)
    select = member[:, None, :] & (rank[:, None, :] == slot[None, :, None])
    select = select.reshape(groups * capacity, rows).astype(int_rows.dtype)
    return jnp.dot(select, int_rows, preferred_element_type=jnp.float32).astype(int_rows.dtype)


def body(amplitudes, cycle_ints, int_rows, row_dest, vir_energy, occ_energy):
    groups = lax.axis_size("pair")
    row_count, local_width = amplitudes.shape
    full_width = local_width * lax.axis_size("vir")
    capacity = SLOTS // groups
    gathered = lax.all_gather(amplitudes, "vir", axis=1, tiled=True)
    cross_part = lax.dot_general(
        gathered, cycle_ints, (((0,), (0,)), ((), ())), preferred_element_type=jnp.float32
    )
    scale_cycle = math.sqrt(row_count * groups * full_width)
    cross_half = lax.psum((cross_part / scale_cycle).astype(jnp.bfloat16), "pair")
    outgoing = dispatch(int_rows, row_dest, groups, capacity)
    arrived = lax.all_to_all(
        outgoing.reshape(groups, capacity, local_width),
        "pair",
        split_axis=0,
        concat_axis=0,
        tiled=True,
    ).reshape(groups * capacity, local_width)
    chosen = lax.all_gather(arrived, "vir", axis=1, tiled=True)
    coefficient = lax.dot_general(
        gathered, chosen, (((1,), (1,)), ((), ())), preferred_element_type=jnp.float32
    ) / math.sqrt(full_width)
    ladder = jnp.dot(
        coefficient.astype(jnp.bfloat16), arrived, preferred_element_type=jnp.float32
    ) / math.sqrt(SLOTS)
    energy = (vir_energy[None, :] - occ_energy[:, None]) * amplitudes.astype(jnp.float32)
    cycle_term = jnp.dot(gathered, cross_half, preferred_element_type=jnp.float32)
    return (cycle_term + ladder + energy).astype(jnp.bfloat16)


def solution(mesh):
    return jax.shard_map(
        body,
        mesh=mesh,
        in_specs=(
            P("pair", "vir"),
            P("pair", "vir"),
            P("pair", "vir"),
            P("pair", None),
            P("vir"),
            P("pair"),
        ),
        out_specs=P("pair", "vir"),
        check_vma=False,
    )
```

profile of v0, /device:TPU:0, one launch (start us, length us, event | category | flops | bytes accessed | tf_op | source)
XLA Modules:
  0.0 178.0 jit_solution(11613272002490482271)
XLA Ops:
  6.5 0.0 copy-start
  6.5 0.0 all-gather.2.cloned.1.call-start
  6.5 0.7 all-gather.2.cloned.1.call-update
  7.3 0.0 all-reduce.2.cloned.1.call-start
  7.3 0.1 eq.39
  7.4 0.7 fusion.4
  8.1 0.0 copy-start.1
  8.1 18.8 %all-gather.2.cloned.1.call-done = bf16[2560,1024]{1,0:T(8,128)(2,1)} async-done(((bf16[2560,512]{1,0:T(8,128)(2,1)}), bf16[2560,1024]{1,0:T(8,128)(2,1)}) %all-gather.2.cloned.1.call-update) | async-done | bytes 5242896 | tf_op jit(solution)/shard_map/all_gather | solution.py:29
  26.9 0.0 copy-done
  26.9 6.4 %multiply_convert_fusion = bf16[1024,512]{1,0:T(8,128)(2,1)} fusion(bf16[2560,1024]{1,0:T(8,128)(2,1)} %all-gather.2.cloned.1.call-done, bf16[2560,512]{1,0:T(8,128)(2,1)S(1)} %copy-done), kind=kOutput, calls=%fused_computation.5 | convolution fusion | flops 2685403136 | bytes 8912896 | tf_op jit(solution)/shard_map/dot_general | solution.py:30
  33.3 0.0 all-reduce.2.cloned.1.call-update
  33.3 0.1 convolution_convert_fusion.1
  33.4 0.1 fusion.3
  33.5 0.0 copy-done.1
  33.5 0.9 convolution_convert_fusion
  34.4 6.8 %all-to-all-start = ((bf16[16,16,512]{2,1,0:T(8,128)(2,1)}), bf16[16,16,512]{2,1,0:T(8,128)(2,1)S(1)}, u32[]{:S(2)}, u32[]{:S(2)}) async-start(bf16[16,16,512]{2,1,0:T(8,128)(2,1)} %bitcast.3), calls=%async_computation | async-start | bytes 524288 | tf_op jit(solution)/shard_map/all_to_all | solution.py:36
  41.2 4.4 %copy.12 = bf16[2560,512]{0,1:T(8,128)(2,1)} copy(bf16[2560,512]{1,0:T(8,128)(2,1)} %param.6) | data formatting | bytes 5242880 | tf_op args[0]
  45.6 9.9 %all-to-all-done = bf16[16,16,512]{2,1,0:T(8,128)(2,1)S(1)} async-done(((bf16[16,16,512]{2,1,0:T(8,128)(2,1)}), bf16[16,16,512]{2,1,0:T(8,128)(2,1)S(1)}, u32[]{:S(2)}, u32[]{:S(2)}) %all-to-all-start) | async-done | bytes 262176 | tf_op jit(solution)/shard_map/all_to_all | solution.py:36
  55.5 2.2 %all_gather.7 = bf16[256,1024]{1,0:T(8,128)(2,1)S(1)} all-gather(bf16[256,512]{1,0:T(8,128)(2,1)S(1)} %bitcast.24), channel_id=1, replica_groups=mesh['pair'=16,'vir'=2] {'vir'}, dimensions={1}, use_global_device_ids=true | all-gather | bytes 786432 | tf_op jit(solution)/shard_map/all_gather | solution.py:43
  57.7 0.0 copy-start.2
  57.7 0.0 copy-start.3
  57.7 92.0 %all-reduce.2.cloned.1.call-done = bf16[1024,512]{1,0:T(8,128)(2,1)} async-done(((bf16[1024,512]{1,0:T(8,128)(2,1)}), bf16[1024,512]{1,0:T(8,128)(2,1)}) %all-reduce.2.cloned.1.call-update) | async-done | bytes 1048592 | tf_op jit(solution)/shard_map/psum | solution.py:34
  149.7 8.1 %fusion.6 = f32[512,2560]{1,0:T(8,128)} fusion(bf16[1024,512]{1,0:T(8,128)(2,1)} %all-reduce.2.cloned.1.call-done, bf16[2560,1024]{1,0:T(8,128)(2,1)} %all-gather.2.cloned.1.call-done), kind=kOutput, calls=%fused_computation.14 | convolution fusion | flops 2684354560 | bytes 11534336 | tf_op jit(solution)/shard_map/dot_general | solution.py:51
  157.8 0.0 copy-done.2
  157.8 0.0 copy-done.3
  157.8 9.0 %fusion.1 = bf16[2560,512]{0,1:T(8,128)(2,1)} fusion(f32[512,2560]{1,0:T(8,128)} %fusion.6, bf16[2560,512]{0,1:T(8,128)(2,1)} %copy.12, bf16[256,512]{1,0:T(8,128)(2,1)S(1)} %bitcast.25, f32[2560]{0:T(1024)S(1)} %copy-done.2, f32[512]{0:T(512)S(1)} %copy-done.3, bf16[256,1024]{1,0:T(8,128)(2,1)S(1)} %all_gather.7, ...), kind=kOutput, calls=%fused_computation.2 | convolution fusion | flops 2023751680 | bytes 16527360 | tf_op jit(solution)/shard_map/dot_general | solution.py:47
  166.8 4.4 %copy.13 = bf16[2560,512]{1,0:T(8,128)(2,1)} copy(bf16[2560,512]{0,1:T(8,128)(2,1)} %fusion.1) | data formatting | bytes 5242880 | tf_op jit(solution)/shard_map/convert_element_type | solution.py:52
  (1 shorter events, 0.0 us)
Async XLA Ops:
  6.5 20.3 %copy-start = (bf16[2560,512]{1,0:T(8,128)(2,1)S(1)}, bf16[2560,512]{1,0:T(8,128)(2,1)}, u32[]{:S(2)}) copy-start(bf16[2560,512]{1,0:T(8,128)(2,1)} %param.7) | copy-start | bytes 7864324
  6.5 20.3 %all-gather.2.cloned.1.call-start = ((), (), s32[]{:S(2)}) async-start(), calls=%async_computation.1 | async-start | bytes 7864320 | tf_op jit(solution)/shard_map/all_gather | solution.py:29
  7.3 142.4 %all-reduce.2.cloned.1.call-start = ((), (), s32[]{:S(2)}) async-start(), calls=%async_computation.2 | async-start | bytes 2097152 | tf_op jit(solution)/shard_map/psum | solution.py:34
  8.1 25.4 %copy-start.1 = (bf16[64,512]{1,0:T(8,128)(2,1)S(1)}, bf16[64,512]{1,0:T(8,128)(2,1)}, u32[]{:S(2)}) copy-start(bf16[64,512]{1,0:T(8,128)(2,1)} %param.8) | copy-start | bytes 196612
  34.4 21.1 %all-to-all-start = ((bf16[16,16,512]{2,1,0:T(8,128)(2,1)}), bf16[16,16,512]{2,1,0:T(8,128)(2,1)S(1)}, u32[]{:S(2)}, u32[]{:S(2)}) async-start(bf16[16,16,512]{2,1,0:T(8,128)(2,1)} %bitcast.3), calls=%async_computation | async-start | bytes 524288 | tf_op jit(solution)/shard_map/all_to_all | solution.py:36
  57.7 100.1 %copy-start.2 = (f32[2560]{0:T(1024)S(1)}, f32[2560]{0:T(1024)}, u32[]{:S(2)}) copy-start(f32[2560]{0:T(1024)} %param.11) | copy-start | bytes 30724
  57.7 100.1 %copy-start.3 = (f32[512]{0:T(512)S(1)}, f32[512]{0:T(512)}, u32[]{:S(2)}) copy-start(f32[512]{0:T(512)} %param.10) | copy-start | bytes 6148
Sparse Core Ops, SparseCore 0:
  8.9 17.9 all-gather.1
  33.4 116.2 all-reduce.1
where the time goes:
time: 178 us
  waiting for transfers between devices  121 us (68%)
  matrix products  24.5 us (14%)
  between operations  13.4 us (8%)
  local copies, waits for them, and re-layouts  8.86 us (5%)
  starting transfers between devices  6.82 us (4%)
  blocking collectives  2.17 us (1%)
    psum x1, waiting for transfers between devices, body(): lax.psum((cross_part / scale_cycle).astype(jnp.bfloat16), 'pair')  92 us
    all_gather x1, waiting for transfers between devices, body(): gathered = lax.all_gather(amplitudes, 'vir', axis=1, tiled=True)  18.8 us
    all_to_all x1, waiting for transfers between devices, body(): lax.all_to_all(outgoing.reshape(groups, capacity, local_width), 'pair', s...  9.9 us
    dot_general x1, matrix products, body(): jnp.dot(coefficient.astype(jnp.bfloat16), arrived, preferred_element_type...  9.01 us
    dot_general x1, matrix products, body(): jnp.dot(gathered, cross_half, preferred_element_type=jnp.float32)  8.08 us
    all_to_all x1, starting transfers between devices, body(): lax.all_to_all(outgoing.reshape(groups, capacity, local_width), 'pair', s...  6.78 us
    dot_general x1, matrix products, body(): lax.dot_general(gathered, cycle_ints, (((0,), (0,)), ((), ())), preferred...  6.4 us
    unnamed x9, local copies, waits for them, and re-layouts  4.4 us
  transfers between devices with their start and end apart: 3, of which 3 were waited for; matrix products, arithmetic and copies ran while one was open for 4% of the time, Pallas kernels for 0%

commit v1 on v0

--- a/solution.py
+++ b/solution.py
@@ -31,7 +31,9 @@
         gathered, cycle_ints, (((0,), (0,)), ((), ())), preferred_element_type=jnp.float32
     )
     scale_cycle = math.sqrt(row_count * groups * full_width)
-    cross_half = lax.psum((cross_part / scale_cycle).astype(jnp.bfloat16), "pair")
+    cross_half = jnp.sum(
+        lax.all_gather((cross_part / scale_cycle).astype(jnp.bfloat16), "pair"), axis=0
+    )
     outgoing = dispatch(int_rows, row_dest, groups, capacity)
     arrived = lax.all_to_all(
         outgoing.reshape(groups, capacity, local_width),

time: 178 us -> 268 us (1.51)
  waiting for transfers between devices: 121 us -> 201 us
  other arithmetic: 0.8 us -> 10 us
    all_gather x0 -> x1, waiting for transfers between devices: none -> 172 us  [body(): lax.all_gather((cross_part / scale_cycle).astype(jnp.bfloat16), 'pair')]
    psum x1 -> x0, waiting for transfers between devices: 92 us -> none  [body(): lax.psum((cross_part / scale_cycle).astype(jnp.bfloat16), 'pair')]
    reduce_sum x0 -> x1, other arithmetic: none -> 9.92 us  [body(): jnp.sum(lax.all_gather((cross_part / scale_cycle).astype(jnp.bfloat16), '...]
  transfers between devices with their start and end apart: 3 -> 3, of which waited for: 3 -> 3; matrix products, arithmetic and copies ran while one was open for 4% -> 2% of each run, Pallas kernels for 0% -> 0%
where the time goes in v1:
time: 268 us; the launch traced here: 267 us
  waiting for transfers between devices  201 us (75%)
  matrix products  24.5 us (9%)
  between operations  13.5 us (5%)
  other arithmetic  10 us (4%)
  local copies, waits for them, and re-layouts  9.01 us (3%)
  starting transfers between devices  6.82 us (3%)
    all_gather x1, waiting for transfers between devices, body(): lax.all_gather((cross_part / scale_cycle).astype(jnp.bfloat16), 'pair')  172 us
    all_gather x1, waiting for transfers between devices, body(): gathered = lax.all_gather(amplitudes, 'vir', axis=1, tiled=True)  19.5 us
    reduce_sum x1, other arithmetic, body(): jnp.sum(lax.all_gather((cross_part / scale_cycle).astype(jnp.bfloat16), '...  9.92 us
    all_to_all x1, waiting for transfers between devices, body(): lax.all_to_all(outgoing.reshape(groups, capacity, local_width), 'pair', s...  9.33 us
    dot_general x1, matrix products, body(): jnp.dot(coefficient.astype(jnp.bfloat16), arrived, preferred_element_type...  8.98 us
    dot_general x1, matrix products, body(): jnp.dot(gathered, cross_half, preferred_element_type=jnp.float32)  8.07 us
    all_to_all x1, starting transfers between devices, body(): lax.all_to_all(outgoing.reshape(groups, capacity, local_width), 'pair', s...  6.78 us
    dot_general x1, matrix products, body(): lax.dot_general(gathered, cycle_ints, (((0,), (0,)), ((), ())), preferred...  6.4 us
  transfers between devices with their start and end apart: 3, of which 3 were waited for; matrix products, arithmetic and copies ran while one was open for 2% of the time, Pallas kernels for 0%

profile of v1, /device:TPU:0, one launch (start us, length us, event | category | flops | bytes accessed | tf_op | source)
XLA Modules:
  0.0 267.2 jit_solution(10140457295716276871)
XLA Ops:
  6.5 0.0 copy-start
  6.5 0.0 all-gather.4.cloned.1.call-start
  6.5 0.7 all-gather.4.cloned.1.call-update
  7.3 0.0 copy-start.2
  7.3 0.0 copy-start.1
  7.3 0.0 all-gather.6.cloned.1.call-start
  7.3 19.5 %all-gather.4.cloned.1.call-done = bf16[2560,1024]{1,0:T(8,128)(2,1)} async-done(((bf16[2560,512]{1,0:T(8,128)(2,1)}), bf16[2560,1024]{1,0:T(8,128)(2,1)}) %all-gather.4.cloned.1.call-update) | async-done | bytes 5242896 | tf_op jit(solution)/shard_map/all_gather | solution.py:29
  26.9 0.0 copy-done
  26.9 6.4 %multiply_convert_fusion = bf16[1024,512]{1,0:T(8,128)(2,1)} fusion(bf16[2560,1024]{1,0:T(8,128)(2,1)} %all-gather.4.cloned.1.call-done, bf16[2560,512]{1,0:T(8,128)(2,1)S(1)} %copy-done), kind=kOutput, calls=%fused_computation.5 | convolution fusion | flops 2685403136 | bytes 8912896 | tf_op jit(solution)/shard_map/dot_general | solution.py:30
  33.3 0.0 all-gather.6.cloned.1.call-update
  33.3 0.1 eq.39
  33.4 0.0 copy-done.2
  33.4 0.1 convolution_convert_fusion.1
  33.5 0.1 fusion.3
  33.6 0.0 copy-done.1
  33.6 0.9 convolution_convert_fusion
  34.5 6.8 %all-to-all-start = ((bf16[16,16,512]{2,1,0:T(8,128)(2,1)}), bf16[16,16,512]{2,1,0:T(8,128)(2,1)S(1)}, u32[]{:S(2)}, u32[]{:S(2)}) async-start(bf16[16,16,512]{2,1,0:T(8,128)(2,1)} %bitcast.4), calls=%async_computation | async-start | bytes 524288 | tf_op jit(solution)/shard_map/all_to_all | solution.py:38
  41.3 4.5 %copy.12 = bf16[2560,512]{0,1:T(8,128)(2,1)} copy(bf16[2560,512]{1,0:T(8,128)(2,1)} %param.6) | data formatting | bytes 5242880 | tf_op args[0]
  45.9 9.3 %all-to-all-done = bf16[16,16,512]{2,1,0:T(8,128)(2,1)S(1)} async-done(((bf16[16,16,512]{2,1,0:T(8,128)(2,1)}), bf16[16,16,512]{2,1,0:T(8,128)(2,1)S(1)}, u32[]{:S(2)}, u32[]{:S(2)}) %all-to-all-start) | async-done | bytes 262176 | tf_op jit(solution)/shard_map/all_to_all | solution.py:38
  55.2 2.2 all_gather.15
  57.4 171.7 %all-gather.6.cloned.1.call-done = bf16[16384,512]{1,0:T(8,128)(2,1)} async-done(((bf16[1024,512]{1,0:T(8,128)(2,1)}), bf16[16384,512]{1,0:T(8,128)(2,1)}) %all-gather.6.cloned.1.call-update) | async-done | bytes 16777232 | tf_op jit(solution)/shard_map/all_gather | solution.py:35
  229.0 9.9 %reduce_sum.12 = bf16[1024,512]{1,0:T(8,128)(2,1)} reduce(bf16[16,1024,512]{2,1,0:T(8,128)(2,1)} %bitcast.25, bf16[]{:T(256)} %constant.10.clone.1), dimensions={0}, to_apply=%region_0.0 | reduce | flops 7864320 | bytes 17825794 | tf_op jit(solution)/shard_map/reduce_sum | solution.py:34
  238.9 0.0 copy-start.3
  238.9 0.0 copy-start.4
  238.9 8.1 %fusion.6 = f32[512,2560]{1,0:T(8,128)} fusion(bf16[1024,512]{1,0:T(8,128)(2,1)} %reduce_sum.12, bf16[2560,1024]{1,0:T(8,128)(2,1)} %all-gather.4.cloned.1.call-done), kind=kOutput, calls=%fused_computation.14 | convolution fusion | flops 2684354560 | bytes 11534336 | tf_op jit(solution)/shard_map/dot_general | solution.py:53
  247.0 0.0 copy-done.3
  247.0 0.0 copy-done.4
  247.0 9.0 %fusion.1 = bf16[2560,512]{0,1:T(8,128)(2,1)} fusion(f32[512,2560]{1,0:T(8,128)} %fusion.6, bf16[2560,512]{0,1:T(8,128)(2,1)} %copy.12, bf16[256,512]{1,0:T(8,128)(2,1)S(1)} %bitcast.27, f32[2560]{0:T(1024)S(1)} %copy-done.3, f32[512]{0:T(512)S(1)} %copy-done.4, bf16[256,1024]{1,0:T(8,128)(2,1)S(1)} %all_gather.15, ...), kind=kOutput, calls=%fused_computation.2 | convolution fusion | flops 2023751680 | bytes 16527360 | tf_op jit(solution)/shard_map/dot_general | solution.py:49
  256.0 4.4 %copy.13 = bf16[2560,512]{1,0:T(8,128)(2,1)} copy(bf16[2560,512]{0,1:T(8,128)(2,1)} %fusion.1) | data formatting | bytes 5242880 | tf_op jit(solution)/shard_map/convert_element_type | solution.py:54
  (2 shorter events, 0.0 us)
Async XLA Ops:
  6.5 20.3 %copy-start = (bf16[2560,512]{1,0:T(8,128)(2,1)S(1)}, bf16[2560,512]{1,0:T(8,128)(2,1)}, u32[]{:S(2)}) copy-start(bf16[2560,512]{1,0:T(8,128)(2,1)} %param.7) | copy-start | bytes 7864324
  6.5 20.3 %all-gather.4.cloned.1.call-start = ((), (), s32[]{:S(2)}) async-start(), calls=%async_computation.1 | async-start | bytes 7864320 | tf_op jit(solution)/shard_map/all_gather | solution.py:29
  7.3 26.1 %copy-start.2 = (s32[64,2]{0,1:T(2,128)S(1)}, s32[64,2]{0,1:T(2,128)}, u32[]{:S(2)}) copy-start(s32[64,2]{0,1:T(2,128)} %param.9) | copy-start | bytes 1540
  7.3 26.4 %copy-start.1 = (bf16[64,512]{1,0:T(8,128)(2,1)S(1)}, bf16[64,512]{1,0:T(8,128)(2,1)}, u32[]{:S(2)}) copy-start(bf16[64,512]{1,0:T(8,128)(2,1)} %param.8) | copy-start | bytes 196612
  7.3 221.7 %all-gather.6.cloned.1.call-start = ((), (), s32[]{:S(2)}) async-start(), calls=%async_computation.2 | async-start | bytes 17825792 | tf_op jit(solution)/shard_map/all_gather | solution.py:35
  34.5 20.6 %all-to-all-start = ((bf16[16,16,512]{2,1,0:T(8,128)(2,1)}), bf16[16,16,512]{2,1,0:T(8,128)(2,1)S(1)}, u32[]{:S(2)}, u32[]{:S(2)}) async-start(bf16[16,16,512]{2,1,0:T(8,128)(2,1)} %bitcast.4), calls=%async_computation | async-start | bytes 524288 | tf_op jit(solution)/shard_map/all_to_all | solution.py:38
  238.9 8.1 %copy-start.3 = (f32[2560]{0:T(1024)S(1)}, f32[2560]{0:T(1024)}, u32[]{:S(2)}) copy-start(f32[2560]{0:T(1024)} %param.11) | copy-start | bytes 30724
  238.9 8.1 %copy-start.4 = (f32[512]{0:T(512)S(1)}, f32[512]{0:T(512)}, u32[]{:S(2)}) copy-start(f32[512]{0:T(512)} %param.10) | copy-start | bytes 6148
Sparse Core Ops, SparseCore 0:
  8.9 17.9 all-gather.3
  33.4 195.5 all-gather.5
